TPU v7x, 128 devices: a whole 4x4x4 slice. The times are simulated.
128 devices in a mesh: dp: 2 (over x_lo), tm: 64 (over z, y, x_hi, core).
Axes of the slice: x: 4 (x_hi: 2, x_lo: 2; x = x_hi * 2 + x_lo), y: 4, z: 4, core: 2. Of those that a mesh axis runs over, the one named last changes fastest.
Arguments:
- frames: bfloat16 [2, 64, 36, 64, 640], P('dp', 'tm'), may hold values from -8 to 8
- norm_gain: float32 [640], replicated, may hold values from 0.1 to 1.9
- norm_shift: float32 [640], replicated, may hold values from -1.5 to 1.5
- spatial_weight: bfloat16 [3, 3, 640, 640], P(None, None, 'dp'), may hold values from -0.078125 to 0.078125
- spatial_bias: float32 [640], replicated, may hold values from -1.5 to 1.5
- temporal_weight: bfloat16 [3, 640, 640], P(None, 'dp'), may hold values from -0.125 to 0.125
- temporal_bias: float32 [640], replicated, may hold values from -1.5 to 1.5
Outputs:
- block_out: bfloat16 [2, 64, 36, 64, 640], P('dp', 'tm')
All inputs are finite; a program needn't handle non-finite values.
Results may differ from a plain program's by a relative error of at most 0.006.
Values may be sent and summed in bfloat16 or wider, within the bound.
A program may use at most 192 MiB of HBM per device.

v0:
```python
import jax
import jax.numpy as jnp
from jax import lax
from jax.sharding import PartitionSpec as P

GROUPS = 32


def extended(x, sides, width):
    for axis, dim in sides:
        count, length = (lax.axis_size(axis), x.shape[dim])
        up = [(i, (i + 1) % count) for i in range(count - 1)]
        down = [(j, i) for i, j in up]
        last = lax.slice_in_dim(x, length - width, length, axis=dim)
        leading = lax.slice_in_dim(x, 0, width, axis=dim)
        before = lax.ppermute(last, axis, up)
        after = lax.ppermute(leading, axis, down)
        x = jnp.concatenate([before, x, after], axis=dim)
    return x


def shards(
    frames, norm_gain, norm_shift, spatial_weight, spatial_bias, temporal_weight, temporal_bias
):
    height = frames.shape[2]
    columns = frames.shape[3]
    channels = frames.shape[4]
    per_group = channels // GROUPS
    temporal_full = lax.all_gather(temporal_weight, "dp", axis=1, tiled=True)
    signal = frames[0, 0].astype(jnp.float32)
    grouped = signal.reshape(height, columns, GROUPS, per_group)
    sum_values, sum_squares = lax.psum(
        (jnp.sum(grouped, axis=(0, 1, 3)), jnp.sum(grouped * grouped, axis=(0, 1, 3))), "tm"
    )
    members = lax.axis_size("tm") * height * columns * per_group
    average = sum_values / members
    variance = sum_squares / members - average * average
    inverse_std = lax.rsqrt(variance + 1e-05)
    normed = ((grouped - average[:, None]) * inverse_std[:, None]).reshape(
        height, columns, channels
    )
    hidden = jax.nn.silu(normed * norm_gain + norm_shift).astype(jnp.bfloat16)
    padded = jnp.pad(hidden, ((1, 1), (1, 1), (0, 0)))
    empty = jnp.zeros((height * columns, channels), jnp.float32)
    spatial_full = lax.all_gather(spatial_weight, "dp", axis=2, tiled=True)
    running = empty
    section_width = spatial_full.shape[2]
    for row_tap in range(3):
        for col_tap in range(3):
            window = padded[row_tap : row_tap + height, col_tap : col_tap + columns].reshape(
                height * columns, section_width
            )
            running = running + jnp.dot(
                window, spatial_full[row_tap, col_tap], preferred_element_type=jnp.float32
            )
    spatial = (running + spatial_bias).astype(jnp.bfloat16).reshape(height, columns, channels)
    stacked = extended(spatial[None], (("tm", 0),), 1)
    mixed = jnp.einsum("khwc,kcd->hwd", stacked, temporal_full, preferred_element_type=jnp.float32)
    block_out = (signal + mixed + temporal_bias).astype(jnp.bfloat16)
    return block_out[None, None]


def solution(mesh):
    in_specs = (
        P("dp", "tm", None, None, None),
        P(),
        P(),
        P(None, None, "dp", None),
        P(),
        P(None, "dp", None),
        P(),
    )
    out_specs = P("dp", "tm", None, None, None)
    return jax.shard_map(shards, mesh=mesh, in_specs=in_specs, out_specs=out_specs, check_vma=False)
```

profile of v0, /device:TPU:1, one launch (start us, length us, event | category | flops | bytes accessed | tf_op | source)
XLA Modules:
  0.0 363.7 jit_solution(4455475468057267332)
XLA Ops:
  6.5 0.7 all-gather.3.cloned.1.call-update
  7.3 2.9 convert_reduce_fusion
  10.4 0.1 reduce_sum.25
  10.5 0.1 reduce_sum.37
  10.6 165.9 %all-reduce.1 = (f32[32]{0:T(128)S(1)}, f32[32]{0:T(128)S(1)}) all-reduce(f32[32]{0:T(128)S(1)} %reduce_sum.37, f32[32]{0:T(128)S(1)} %reduce_sum.25), channel_id=1, replica_groups=mesh['dp'=2,'tm'=64] {'tm'}, use_global_device_ids=true, to_apply=%region_5.6 | all-reduce | flops 64 | bytes 512 | tf_op jit(solution)/shard_map/psum | solution.py:32
  176.6 0.1 mul.51
  176.9 2.1 fusion.16
  179.0 10.8 %pad_slice_fusion = (bf16[36,64,640]{2,1,0:T(8,128)(2,1)}, bf16[36,64,640]{2,1,0:T(8,128)(2,1)}, bf16[36,64,640]{2,1,0:T(8,128)(2,1)}, bf16[36,64,640]{2,1,0:T(8...) fusion(bf16[36,64,640]{2,1,0:T(8,128)(2,1)S(1)} %fusion.16), kind=kLoop, calls=%fused_computation.35 | loop fusion | bytes 26542080 | tf_op jit(solution)/shard_map/slice | solution.py:50
  189.9 3.2 fusion.28
  193.1 7.5 %fusion.33 = f32[2304,640]{1,0:T(8,128)} fusion(bf16[2304,640]{1,0:T(8,128)(2,1)} %bitcast.99, bf16[3,3,640,640]{3,2,1,0:T(8,128)(2,1)} %all-gather.3.cloned.1.call-done), kind=kOutput, calls=%fused_computation.46 | convolution fusion | flops 1887436800 | bytes 9666560 | tf_op jit(solution)/shard_map/dot_general | solution.py:53
  200.6 4.5 %fusion.34 = f32[2304,640]{1,0:T(8,128)} fusion(bf16[2304,640]{1,0:T(8,128)(2,1)S(1)} %bitcast.98, bf16[3,3,640,640]{3,2,1,0:T(8,128)(2,1)S(1)} %copy-done.8), kind=kOutput, calls=%fused_computation.48 | convolution fusion | flops 1887436800 | bytes 9666560 | tf_op jit(solution)/shard_map/dot_general | solution.py:53
  205.1 4.5 %fusion.35 = f32[2304,640]{1,0:T(8,128)} fusion(bf16[2304,640]{1,0:T(8,128)(2,1)S(1)} %bitcast.97, bf16[3,3,640,640]{3,2,1,0:T(8,128)(2,1)S(1)} %copy-done.8), kind=kOutput, calls=%fused_computation.50 | convolution fusion | flops 1887436800 | bytes 9666560 | tf_op jit(solution)/shard_map/dot_general | solution.py:53
  209.7 4.6 %fusion.37 = f32[2304,640]{1,0:T(8,128)} fusion(bf16[2304,640]{1,0:T(8,128)(2,1)S(1)} %bitcast.96, bf16[3,3,640,640]{3,2,1,0:T(8,128)(2,1)S(1)} %copy-done.8), kind=kOutput, calls=%fused_computation.54 | convolution fusion | flops 1887436800 | bytes 9666560 | tf_op jit(solution)/shard_map/dot_general | solution.py:53
  214.3 4.5 %fusion.38 = f32[2304,640]{1,0:T(8,128)} fusion(bf16[2304,640]{1,0:T(8,128)(2,1)S(1)} %bitcast.95, bf16[3,3,640,640]{3,2,1,0:T(8,128)(2,1)S(1)} %copy-done.8), kind=kOutput, calls=%fused_computation.56 | convolution fusion | flops 1887436800 | bytes 9666560 | tf_op jit(solution)/shard_map/dot_general | solution.py:53
  218.8 4.5 %fusion.39 = f32[2304,640]{1,0:T(8,128)} fusion(bf16[2304,640]{1,0:T(8,128)(2,1)S(1)} %bitcast.94, bf16[3,3,640,640]{3,2,1,0:T(8,128)(2,1)S(1)} %copy-done.8), kind=kOutput, calls=%fused_computation.58 | convolution fusion | flops 1887436800 | bytes 9666560 | tf_op jit(solution)/shard_map/dot_general | solution.py:53
  223.3 4.5 %fusion.40 = f32[2304,640]{1,0:T(8,128)} fusion(bf16[2304,640]{1,0:T(8,128)(2,1)S(1)} %bitcast.93, bf16[3,3,640,640]{3,2,1,0:T(8,128)(2,1)S(1)} %copy-done.8), kind=kOutput, calls=%fused_computation.60 | convolution fusion | flops 1887436800 | bytes 9666560 | tf_op jit(solution)/shard_map/dot_general | solution.py:53
  227.9 4.6 %fusion.36 = f32[2304,640]{1,0:T(8,128)} fusion(bf16[2304,640]{1,0:T(8,128)(2,1)S(1)} %bitcast.103, bf16[3,3,640,640]{3,2,1,0:T(8,128)(2,1)S(1)} %copy-done.8), kind=kOutput, calls=%fused_computation.52 | convolution fusion | flops 1887436800 | bytes 9666560 | tf_op jit(solution)/shard_map/dot_general | solution.py:53
  232.5 21.0 %add_convert_fusion = bf16[2304,640]{1,0:T(8,128)(2,1)} fusion(f32[2304,640]{1,0:T(8,128)} %fusion.33, f32[2304,640]{1,0:T(8,128)} %fusion.34, f32[2304,640]{1,0:T(8,128)} %fusion.35, f32[2304,640]{1,0:T(8,128)} %fusion.36, f32[2304,640]{1,0:T(8,128)} %fusion.37, f32[2304,640]{1,0:T(8,128)} %fusion.38, f32[2304,640]{1,0:T(8,128)} %fusion.40, ...), kind=kOutput, calls=%fused_computation.33 | convolution fusion | flops 1902182400 | bytes 53905920 | tf_op jit(solution)/shard_map/dot_general | solution.py:53
  253.5 4.5 %collective-permute-start = (bf16[1,36,64,640]{3,2,0,1:T(8,128)(2,1)}, bf16[1,36,64,640]{3,2,0,1:T(8,128)(2,1)}, u32[]{:S(2)}, u32[]{:S(2)}) collective-permute-start(bf16[1,36,64,640]{3,2,0,1:T(8,128)(2,1)} %bitcast.100), channel_id=1, source_target_pairs={{0,1},{1,2},{2,3},{3,4},{4,5},{5,6},{6,7},{7,8},{8,9},{9,10},{10,1... | collective-permute-start | bytes 8847368 | tf_op jit(solution)/shard_map/ppermute | solution.py:16
  258.0 7.8 %collective-permute-start.1 = (bf16[1,36,64,640]{3,2,0,1:T(8,128)(2,1)}, bf16[1,36,64,640]{3,2,0,1:T(8,128)(2,1)}, u32[]{:S(2)}, u32[]{:S(2)}) collective-permute-start(bf16[1,36,64,640]{3,2,0,1:T(8,128)(2,1)} %bitcast.101), channel_id=1, source_target_pairs={{1,0},{2,1},{3,2},{4,3},{5,4},{6,5},{7,6},{8,7},{9,8},{10,9},{11,1... | collective-permute-start | bytes 8847368 | tf_op jit(solution)/shard_map/ppermute | solution.py:17
  265.8 46.6 %all-gather.5.cloned.1.call-done = bf16[3,640,640]{2,1,0:T(8,128)(2,1)} async-done(((bf16[3,320,640]{2,1,0:T(8,128)(2,1)}), bf16[3,640,640]{2,1,0:T(8,128)(2,1)}) %all-gather.5.cloned.1.call-update) | async-done | bytes 2457616 | tf_op jit(solution)/shard_map/all_gather | solution.py:29
  312.4 4.4 %collective-permute-done = bf16[1,36,64,640]{3,2,0,1:T(8,128)(2,1)} collective-permute-done((bf16[1,36,64,640]{3,2,0,1:T(8,128)(2,1)}, bf16[1,36,64,640]{3,2,0,1:T(8,128)(2,1)}, u32[]{:S(2)}, u32[]{:S(2)}) %collective-permute-start) | collective-permute-done | bytes 2949152 | tf_op jit(solution)/shard_map/ppermute | solution.py:16
  316.7 28.2 %collective-permute-done.1 = bf16[1,36,64,640]{3,2,0,1:T(8,128)(2,1)} collective-permute-done((bf16[1,36,64,640]{3,2,0,1:T(8,128)(2,1)}, bf16[1,36,64,640]{3,2,0,1:T(8,128)(2,1)}, u32[]{:S(2)}, u32[]{:S(2)}) %collective-permute-start.1) | collective-permute-done | bytes 2949152 | tf_op jit(solution)/shard_map/ppermute | solution.py:17
  345.0 11.9 %fusion.29 = bf16[1,1,36,64,640]{4,3,2,1,0:T(8,128)(2,1)} fusion(bf16[1,1,36,64,640]{4,3,2,1,0:T(8,128)(2,1)S(1)} %copy-done, f32[640]{0:T(1024)S(1)} %copy-done.12, bf16[1,36,64,640]{3,2,0,1:T(8,128)(2,1)} %collective-permute-done.1, bf16[1,36,64,640]{3,2,0,1:T(8,128)(2,1)} %bitcast.102, bf16[1,36,64,640]{3,2,0,1:T(8,128)(2,1)} %collective-permute-done, ...), kind=kOutput, calls=%fused_computation.34 | convolution fusion | flops 5677056000 | bytes 17205760 | tf_op jit(solution)/shard_map/khwc,kcd->hwd/dot_general | solution.py:58
  (36 shorter events, 0.6 us)
Async XLA Ops:
  6.5 170.3 %copy-start = (bf16[1,1,36,64,640]{4,3,2,1,0:T(8,128)(2,1)S(1)}, bf16[1,1,36,64,640]{4,3,2,1,0:T(8,128)(2,1)}, u32[]{:S(2)}) copy-start(bf16[1,1,36,64,640]{4,3,2,1,0:T(8,128)(2,1)} %param.7) | copy-start | bytes 8847364
  6.5 170.3 %copy-start.10 = (f32[640]{0:T(1024)S(1)}, f32[640]{0:T(1024)}, u32[]{:S(2)}) copy-start(f32[640]{0:T(1024)} %param.8) | copy-start | bytes 7684
  6.5 170.3 %copy-start.9 = (f32[640]{0:T(1024)S(1)}, f32[640]{0:T(1024)}, u32[]{:S(2)}) copy-start(f32[640]{0:T(1024)} %param.9) | copy-start | bytes 7684
  6.5 186.5 %all-gather.3.cloned.1.call-start = ((), (), s32[]{:S(2)}) async-start(), calls=%async_computation | async-start | bytes 11059200 | tf_op jit(solution)/shard_map/all_gather | solution.py:45
  7.3 305.1 %all-gather.5.cloned.1.call-start = ((), (), s32[]{:S(2)}) async-start(), calls=%async_computation.1 | async-start | bytes 3686400 | tf_op jit(solution)/shard_map/all_gather | solution.py:29
  193.1 7.5 %copy-start.6 = (bf16[36,64,640]{2,1,0:T(8,128)(2,1)S(1)}, bf16[36,64,640]{2,1,0:T(8,128)(2,1)}, u32[]{:S(2)}) copy-start(bf16[36,64,640]{2,1,0:T(8,128)(2,1)} %get-tuple-element.14) | copy-start | bytes 8847364
  193.1 7.5 %copy-start.8 = (bf16[3,3,640,640]{3,2,1,0:T(8,128)(2,1)S(1)}, bf16[3,3,640,640]{3,2,1,0:T(8,128)(2,1)}, u32[]{:S(2)}) copy-start(bf16[3,3,640,640]{3,2,1,0:T(8,128)(2,1)} %all-gather.3.cloned.1.call-done) | copy-start | bytes 22118404
  200.6 4.6 %copy-start.5 = (bf16[36,64,640]{2,1,0:T(8,128)(2,1)S(1)}, bf16[36,64,640]{2,1,0:T(8,128)(2,1)}, u32[]{:S(2)}) copy-start(bf16[36,64,640]{2,1,0:T(8,128)(2,1)} %get-tuple-element.13) | copy-start | bytes 8847364
  205.1 4.5 %copy-start.4 = (bf16[36,64,640]{2,1,0:T(8,128)(2,1)S(1)}, bf16[36,64,640]{2,1,0:T(8,128)(2,1)}, u32[]{:S(2)}) copy-start(bf16[36,64,640]{2,1,0:T(8,128)(2,1)} %get-tuple-element.12) | copy-start | bytes 8847364
  209.7 4.6 %copy-start.3 = (bf16[36,64,640]{2,1,0:T(8,128)(2,1)S(1)}, bf16[36,64,640]{2,1,0:T(8,128)(2,1)}, u32[]{:S(2)}) copy-start(bf16[36,64,640]{2,1,0:T(8,128)(2,1)} %get-tuple-element.11) | copy-start | bytes 8847364
  214.3 4.5 %copy-start.2 = (bf16[36,64,640]{2,1,0:T(8,128)(2,1)S(1)}, bf16[36,64,640]{2,1,0:T(8,128)(2,1)}, u32[]{:S(2)}) copy-start(bf16[36,64,640]{2,1,0:T(8,128)(2,1)} %get-tuple-element.10) | copy-start | bytes 8847364
  218.8 4.5 %copy-start.1 = (bf16[36,64,640]{2,1,0:T(8,128)(2,1)S(1)}, bf16[36,64,640]{2,1,0:T(8,128)(2,1)}, u32[]{:S(2)}) copy-start(bf16[36,64,640]{2,1,0:T(8,128)(2,1)} %get-tuple-element.16) | copy-start | bytes 8847364
  223.3 4.5 %copy-start.7 = (bf16[1,1,36,64,640]{4,3,2,1,0:T(8,128)(2,1)S(1)}, bf16[1,1,36,64,640]{4,3,2,1,0:T(8,128)(2,1)}, u32[]{:S(2)}) copy-start(bf16[1,1,36,64,640]{4,3,2,1,0:T(8,128)(2,1)} %fusion.28) | copy-start | bytes 8847364
  227.9 4.6 %copy-start.11 = (f32[640]{0:T(1024)S(1)}, f32[640]{0:T(1024)}, u32[]{:S(2)}) copy-start(f32[640]{0:T(1024)} %param.11) | copy-start | bytes 7684
  232.5 112.5 %copy-start.12 = (f32[640]{0:T(1024)S(1)}, f32[640]{0:T(1024)}, u32[]{:S(2)}) copy-start(f32[640]{0:T(1024)} %param.13) | copy-start | bytes 7684
  253.5 63.2 %collective-permute-start = (bf16[1,36,64,640]{3,2,0,1:T(8,128)(2,1)}, bf16[1,36,64,640]{3,2,0,1:T(8,128)(2,1)}, u32[]{:S(2)}, u32[]{:S(2)}) collective-permute-start(bf16[1,36,64,640]{3,2,0,1:T(8,128)(2,1)} %bitcast.100), channel_id=1, source_target_pairs={{0,1},{1,2},{2,3},{3,4},{4,5},{5,6},{6,7},{7,8},{8,9},{9,10},{10,1... | collective-permute-start | bytes 8847368 | tf_op jit(solution)/shard_map/ppermute | solution.py:16
  258.0 86.9 %collective-permute-start.1 = (bf16[1,36,64,640]{3,2,0,1:T(8,128)(2,1)}, bf16[1,36,64,640]{3,2,0,1:T(8,128)(2,1)}, u32[]{:S(2)}, u32[]{:S(2)}) collective-permute-start(bf16[1,36,64,640]{3,2,0,1:T(8,128)(2,1)} %bitcast.101), channel_id=1, source_target_pairs={{1,0},{2,1},{3,2},{4,3},{5,4},{6,5},{7,6},{8,7},{9,8},{10,9},{11,1... | collective-permute-start | bytes 8847368 | tf_op jit(solution)/shard_map/ppermute | solution.py:17
Sparse Core Ops, SparseCore 0:
  9.0 99.6 all-gather.2
  265.9 46.4 all-gather.4
where the time goes:
time: 364 us
  blocking collectives  166 us (46%)
  waiting for transfers between devices  79.9 us (22%)
  matrix products  72.3 us (20%)
  between operations  13.5 us (4%)
  starting transfers between devices  12.3 us (3%)
  local copies, waits for them, and re-layouts  11.4 us (3%)
  other arithmetic  8.43 us (2%)
    psum x1, blocking collectives, shards(): lax.psum((jnp.sum(grouped, axis=(0, 1, 3)), jnp.sum(grouped * grouped, ax...  166 us
    dot_general x9, matrix products, shards(): jnp.dot(window, spatial_full[row_tap, col_tap], preferred_element_type=jn...  60.4 us
    all_gather x1, waiting for transfers between devices, shards(): temporal_full = lax.all_gather(temporal_weight, 'dp', axis=1, tiled=True)  46.6 us
    ppermute x1, waiting for transfers between devices, extended(): after = lax.ppermute(leading, axis, down)  28.2 us
    dot_general x1, matrix products, shards(): jnp.einsum('khwc,kcd->hwd', stacked, temporal_full, preferred_element_typ...  11.9 us
    slice x1, local copies, waits for them, and re-layouts, shards(): padded[row_tap:row_tap + height, col_tap:col_tap + columns]  10.8 us
    ppermute x1, starting transfers between devices, extended(): after = lax.ppermute(leading, axis, down)  7.76 us
  transfers between devices with their start and end apart: 4, of which 3 were waited for; matrix products, arithmetic and copies ran while one was open for 5% of the time, Pallas kernels for 0%

commit v1 on v0

v1 whole, which is shorter than its diff:
```python
import functools

import jax
import jax.numpy as jnp
from jax import lax
from jax.experimental import pallas as pl
from jax.experimental.pallas import tpu as pltpu
from jax.sharding import PartitionSpec as P

MESH = pl.DeviceIdType.MESH
GROUPS = 32
D = 640
H = 36
W = 64
HALF = D // 2
QUART = HALF // 4
R = 4
NCH = H // R
NRAW = 3
M = R * W
MEMBERS = 64 * H * W * (D // GROUPS)


def device(x, y, z, core):
    x, y, z = lax.rem(x + 4, 4), lax.rem(y + 4, 4), lax.rem(z + 4, 4)
    return lax.rem(x, 2), ((z * 4 + y) * 2 + x // 2) * 2 + core


def kernel(
    frames, gain, shift, sw, sb, tw, tb, out,
    xin, xf, sf, so, ss, hid, wts, outv,
    st, rs1, tot1, rs2,
    lsem, wsnd, wrcv, st_snd, st_rcv, raw_snd, raw_rcv, sp_snd, sp_rcv, sib_snd, sib_rcv, out_sem,
):
    dp = lax.axis_index("dp")
    tm = lax.axis_index("tm")
    core = lax.rem(tm, 2)
    xh = lax.rem(tm // 2, 2)
    y = lax.rem(tm // 4, 4)
    z = tm // 16
    x = xh * 2 + dp
    other = 1 - dp

    sibling = (dp, tm + 1 - 2 * core)
    partner = (dp, lax.rem(tm + 2 * core - 1 + 64, 64))
    valid = jnp.logical_and(tm > 0, tm < 63)
    x_to = device(x + 2 * core - 1, y, z, core)
    x_from = device(x + 1 - 2 * core, y, z, core)
    up = device(x, y + 1 - core, z + core, core)
    down = device(x, y - 1 + core, z - core, core)
    pos = y * (1 - core) + z * core
    g1 = y * 2 + core
    g2 = z * 2 + xh

    def first_group(k):
        g = lax.rem(g1 + k, 8)
        return device(x, g // 2, z, lax.rem(g, 2))

    def second_group(k):
        g = lax.rem(g2 + k, 8)
        return device(lax.rem(g, 2) * 2 + dp, y, g // 2, core)

    load_x = pltpu.make_async_copy(frames, xin, lsem.at[0])
    mine = pl.ds(pl.multiple_of(dp * HALF, 16), HALF)
    load_s = pltpu.make_async_copy(sw, wts.at[pl.ds(0, 9), mine, :], lsem.at[1])
    load_t = pltpu.make_async_copy(tw, wts.at[pl.ds(9, 3), mine, :], lsem.at[2])
    load_x.start()
    load_s.start()
    load_t.start()

    barrier = pltpu.get_barrier_semaphore()
    greet = [sibling, partner, x_to, x_from, up, down]
    greet += [first_group(k) for k in range(1, 8)] + [second_group(k) for k in range(1, 8)]
    for who in greet:
        pl.semaphore_signal(barrier, inc=1, device_id=who, device_id_type=MESH)
    pl.semaphore_wait(barrier, len(greet))

    def send(src, dst, ssem, rsem, who):
        return pltpu.make_async_remote_copy(
            src_ref=src, dst_ref=dst, send_sem=ssem, recv_sem=rsem, device_id=who, device_id_type=MESH
        )

    def part(half, owner_core, q, first=0, count=6):
        rows = pl.ds(pl.multiple_of(half * HALF + lax.rem(q + 4, 4) * QUART, 16), QUART)
        return wts.at[pl.ds(owner_core * 6 + first, count), rows, :]

    def wcopy(piece, i, who):
        return send(piece, piece, wsnd.at[i], wrcv.at[i], who)

    load_s.wait()
    load_t.wait()
    x_out = wcopy(part(dp, core, pos), 0, x_to)
    x_out.start()

    load_x.wait()

    def add_rows(i, carry):
        s, q = carry
        v = xin[pl.ds(pl.multiple_of(i * W, W), W), :].astype(jnp.float32).reshape(W // 8, 8, D)
        return s + jnp.sum(v, axis=0), q + jnp.sum(v * v, axis=0)

    zero = jnp.zeros((8, D), jnp.float32)
    s, q = lax.fori_loop(0, H, add_rows, (zero, zero))
    st[0:1, :] = jnp.sum(s, axis=0, keepdims=True)
    st[1:2, :] = jnp.sum(q, axis=0, keepdims=True)
    ones = []
    for k in range(1, 8):
        ones.append(send(st, rs1.at[k - 1], st_snd.at[k - 1], st_rcv.at[k - 1], first_group(k)))
        ones[-1].start()
    hid[0:W, :] = jnp.zeros((W, 3 * D), jnp.bfloat16)
    hid[(H + 1) * W:(H + 2) * W, :] = jnp.zeros((W, 3 * D), jnp.bfloat16)
    for c in ones:
        c.wait_recv()
    tot1[...] = st[...] + jnp.sum(rs1[...], axis=0)
    twos = []
    for k in range(1, 8):
        twos.append(send(tot1, rs2.at[k - 1], st_snd.at[k + 6], st_rcv.at[k + 6], second_group(k)))
        twos[-1].start()
    for c in twos:
        c.wait_recv()
    total = tot1[...] + jnp.sum(rs2[...], axis=0)

    ch = lax.broadcasted_iota(jnp.int32, (D, 128), 0)
    gr = lax.broadcasted_iota(jnp.int32, (D, 128), 1) * (D // GROUPS)
    member = jnp.logical_and(ch >= gr, ch < gr + D // GROUPS).astype(jnp.float32)
    ch_t = lax.broadcasted_iota(jnp.int32, (128, D), 1)
    gr_t = lax.broadcasted_iota(jnp.int32, (128, D), 0) * (D // GROUPS)
    spread = jnp.logical_and(ch_t >= gr_t, ch_t < gr_t + D // GROUPS).astype(jnp.float32)
    eight = jnp.concatenate([total, jnp.zeros((6, D), jnp.float32)], axis=0)
    per_group = jnp.dot(
        eight, member, precision=lax.Precision.HIGHEST, preferred_element_type=jnp.float32
    ) * (1.0 / MEMBERS)
    average = per_group[0:1, :]
    inv = lax.rsqrt(per_group[1:2, :] - average * average + 1e-5)
    pair = jnp.concatenate([average, inv, jnp.zeros((6, 128), jnp.float32)], axis=0)
    pair = jnp.dot(pair, spread, precision=lax.Precision.HIGHEST, preferred_element_type=jnp.float32)
    scale = pair[1:2, :] * gain[...]
    half_scale = scale * 0.5
    half_shift = (shift[...] - pair[0:1, :] * scale) * 0.5
    bias_s = sb[...]
    bias_t = tb[...]

    col = lax.broadcasted_iota(jnp.int32, (W, 128), 0)
    not_first = col > 0
    not_last = col < W - 1

    def normalise_row(src, row):
        base = pl.multiple_of(row * W, W)
        to = pl.ds(pl.multiple_of((row + 1) * W, W), W)
        for b in range(D // 128):
            lanes = slice(b * 128, (b + 1) * 128)
            v = src[pl.ds(base, W), lanes].astype(jnp.float32)
            u = v * half_scale[:, lanes] + half_shift[:, lanes]
            h = u + u * jnp.tanh(u)
            before = jnp.where(not_first, pltpu.roll(h, 1, 0), 0.0)
            after = jnp.where(not_last, pltpu.roll(h, W - 1, 0), 0.0)
            hid[to, lanes] = before.astype(jnp.bfloat16)
            hid[to, D + b * 128:D + (b + 1) * 128] = h.astype(jnp.bfloat16)
            hid[to, 2 * D + b * 128:2 * D + (b + 1) * 128] = after.astype(jnp.bfloat16)

    wcopy(part(other, core, pos), 0, x_to).wait_recv()
    theirs = 1 - core
    ring = [
        wcopy(part(other, core, pos), 1, up),
        wcopy(part(other, core, pos), 2, down),
        wcopy(part(other, core, pos), 5, sibling),
    ]
    for c in ring:
        c.start()

    pre = send(xin.at[pl.ds(0, W), :], xf.at[pl.ds(0, W), :], raw_snd.at[NRAW], raw_rcv.at[NRAW], partner)
    pre.start()

    def raw_copy(i):
        rows = pl.ds(pl.multiple_of(i * M + W, W), M)
        return send(xin.at[rows, :], xf.at[rows, :], raw_snd.at[i], raw_rcv.at[i], partner)

    def start_raw(i, _):
        raw_copy(i).start()
        return 0

    lax.fori_loop(0, NRAW, start_raw, 0)

    def own_row(i, _):
        normalise_row(xin, i)
        return 0

    lax.fori_loop(0, H // 2, own_row, 0)

    wcopy(part(other, core, pos - 1), 1, up).wait_recv()
    more = [wcopy(part(other, core, pos - 1, 0, 3), 3, up), wcopy(part(other, core, pos - 1), 6, sibling)]
    for c in more:
        c.start()
    wcopy(part(other, core, pos + 1), 2, down).wait_recv()
    more2 = [wcopy(part(other, core, pos + 1, 3, 3), 4, down), wcopy(part(other, core, pos + 1), 7, sibling)]
    for c in more2:
        c.start()

    lax.fori_loop(H // 2, H, own_row, 0)

    wcopy(part(other, core, pos + 2, 0, 3), 3, up).wait_recv()
    last = [wcopy(part(other, core, pos + 2, 0, 3), 8, sibling)]
    last[0].start()
    wcopy(part(other, core, pos + 2, 3, 3), 4, down).wait_recv()
    last.append(wcopy(part(other, core, pos + 2, 3, 3), 9, sibling))
    last[1].start()
    their_pos = y * (1 - theirs) + z * theirs
    for piece, i in (
        (part(other, theirs, their_pos), 5),
        (part(other, theirs, their_pos - 1), 6),
        (part(other, theirs, their_pos + 1), 7),
        (part(other, theirs, their_pos + 2, 0, 3), 8),
        (part(other, theirs, their_pos + 2, 3, 3), 9),
    ):
        wcopy(piece, i, sibling).wait_recv()

    def conv(i, dst):
        acc = jnp.broadcast_to(bias_s, (M, D))
        for a in range(3):
            rows = pl.ds(pl.multiple_of(i * M + a * W, W), M)
            acc = acc + jnp.dot(
                hid[rows, :], wts[3 * a:3 * a + 3].reshape(3 * D, D), preferred_element_type=jnp.float32
            )
        dst[pl.ds(pl.multiple_of(i * M, M), M), :] = acc.astype(jnp.bfloat16)

    def chunk(ref, i):
        return ref.at[pl.ds(pl.multiple_of(i * M, M), M), :]

    def to_sibling(i):
        return send(chunk(so, i), chunk(ss, i), sib_snd.at[i], sib_rcv.at[i], sibling)

    def to_partner(i):
        return send(chunk(so, i), chunk(sf, i), sp_snd.at[i], sp_rcv.at[i], partner)

    def shared_chunk(i, _):
        conv(i, so)
        to_partner(i).start()
        to_sibling(i).start()
        return 0

    lax.fori_loop(NRAW, NCH, shared_chunk, 0)

    def own_chunk(i, _):
        conv(i, so)
        to_sibling(i).start()
        return 0

    lax.fori_loop(0, NRAW, own_chunk, 0)

    far_tap = 9 + 2 * core
    near_tap = 11 - 2 * core

    def store(i):
        return pltpu.make_async_copy(chunk(outv, i), chunk(out, i), out_sem.at[i])

    def temporal(i):
        to_sibling(i).wait_recv()
        rows = pl.ds(pl.multiple_of(i * M, M), M)
        acc = xin[rows, :].astype(jnp.float32) + bias_t
        acc = acc + jnp.dot(so[rows, :], wts[10], preferred_element_type=jnp.float32)
        acc = acc + jnp.dot(ss[rows, :], wts[near_tap], preferred_element_type=jnp.float32)
        far = sf[rows, :]
        far = jnp.where(valid, far, jnp.zeros_like(far))
        acc = acc + jnp.dot(far, wts[far_tap], preferred_element_type=jnp.float32)
        outv[rows, :] = acc.astype(jnp.bfloat16)
        store(i).start()

    pre.wait_recv()
    normalise_row(xf, 0)

    def raw_chunk(i, _):
        raw_copy(i).wait_recv()

        def one(j, _):
            normalise_row(xf, i * R + 1 + j)
            return 0

        lax.fori_loop(0, R, one, 0)
        conv(i, sf)
        temporal(i)
        return 0

    lax.fori_loop(0, NRAW, raw_chunk, 0)

    def sent_chunk(i, _):
        to_partner(i).wait_recv()
        temporal(i)
        return 0

    lax.fori_loop(NRAW, NCH, sent_chunk, 0)

    for c in ones + twos + [x_out] + ring + more + more2 + last + [pre]:
        c.wait_send()

    def drain_raw(i, _):
        raw_copy(i).wait_send()
        return 0

    lax.fori_loop(0, NRAW, drain_raw, 0)

    def drain_partner(i, _):
        to_partner(i).wait_send()
        return 0

    lax.fori_loop(NRAW, NCH, drain_partner, 0)

    def drain_all(i, _):
        to_sibling(i).wait_send()
        store(i).wait()
        return 0

    lax.fori_loop(0, NCH, drain_all, 0)


def shards(frames, norm_gain, norm_shift, spatial_weight, spatial_bias, temporal_weight, temporal_bias):
    row = lambda v: v.reshape(1, D)
    vm = pl.BlockSpec(memory_space=pltpu.VMEM)
    hbm = pl.BlockSpec(memory_space=pl.ANY)
    dma = pltpu.SemaphoreType.DMA
    bf = jnp.bfloat16
    result = pl.pallas_call(
        kernel,
        out_shape=jax.ShapeDtypeStruct((H * W, D), bf),
        in_specs=[hbm, vm, vm, hbm, vm, hbm, vm],
        out_specs=hbm,
        scratch_shapes=[
            pltpu.VMEM((H * W, D), bf),
            pltpu.VMEM(((NRAW * R + 1) * W, D), bf),
            pltpu.VMEM((H * W, D), bf),
            pltpu.VMEM((H * W, D), bf),
            pltpu.VMEM((H * W, D), bf),
            pltpu.VMEM(((H + 2) * W, 3 * D), bf),
            pltpu.VMEM((12, D, D), bf),
            pltpu.VMEM((H * W, D), bf),
            pltpu.VMEM((2, D), jnp.float32),
            pltpu.VMEM((7, 2, D), jnp.float32),
            pltpu.VMEM((2, D), jnp.float32),
            pltpu.VMEM((7, 2, D), jnp.float32),
            dma((3,)), dma((10,)), dma((10,)), dma((14,)), dma((14,)),
            dma((NRAW + 1,)), dma((NRAW + 1,)), dma((NCH,)), dma((NCH,)),
            dma((NCH,)), dma((NCH,)), dma((NCH,)),
        ],
        compiler_params=pltpu.CompilerParams(
            collective_id=0, has_side_effects=True, vmem_limit_bytes=56 * 2**20
        ),
    )(
        frames.reshape(H * W, D), row(norm_gain), row(norm_shift),
        spatial_weight.reshape(9, HALF, D), row(spatial_bias), temporal_weight, row(temporal_bias),
    )
    return result.reshape(1, 1, H, W, D)


def solution(mesh):
    in_specs = (
        P("dp", "tm", None, None, None),
        P(),
        P(),
        P(None, None, "dp", None),
        P(),
        P(None, "dp", None),
        P(),
    )
    out_specs = P("dp", "tm", None, None, None)
    return jax.shard_map(shards, mesh=mesh, in_specs=in_specs, out_specs=out_specs, check_vma=False)
```

time: 364 us -> 107 us (0.29)
  the two profiles are of different devices: /device:TPU:1 before, /device:TPU:0 now
where the time goes in v1:
time: 107 us; the launch traced here: 105 us
  Pallas kernels  96.4 us (90%)
  local copies, waits for them, and re-layouts  8.75 us (8%)
    pallas_call x1, Pallas kernels, shards(): pl.pallas_call(kernel, out_shape=jax.ShapeDtypeStruct((H * W, D), bf), in...  96.4 us
    reshape x4, local copies, waits for them, and re-layouts, shards(): row = lambda v: v.reshape(1, D)  5.06 us
    unnamed x1, local copies, waits for them, and re-layouts  3.69 us

profile of v1, /device:TPU:0, one launch (start us, length us, event | category | flops | bytes accessed | tf_op | source)
XLA Modules:
  0.0 105.2 jit_solution(8326322922298027639)
XLA Ops:
  0.0 1.3 %reshape.22.gain = f32[1,640]{1,0:T(1,128)} reshape(f32[640]{0:T(1024)} %param.8) | data formatting | bytes 5120 | tf_op jit(solution)/shard_map/reshape | solution.py:316
  1.3 1.3 %reshape.23.shift = f32[1,640]{1,0:T(1,128)} reshape(f32[640]{0:T(1024)} %param.9) | data formatting | bytes 5120 | tf_op jit(solution)/shard_map/reshape | solution.py:316
  2.5 1.3 %reshape.25.sb = f32[1,640]{1,0:T(1,128)} reshape(f32[640]{0:T(1024)} %param.11) | data formatting | bytes 5120 | tf_op jit(solution)/shard_map/reshape | solution.py:316
  3.8 1.3 %reshape.26.tb = f32[1,640]{1,0:T(1,128)} reshape(f32[640]{0:T(1024)} %param.13) | data formatting | bytes 5120 | tf_op jit(solution)/shard_map/reshape | solution.py:316
  5.1 96.4 %shard_map.73 = bf16[2304,640]{1,0:T(8,128)(2,1)} custom-call(bf16[2304,640]{1,0:T(8,128)(2,1)} %bitcast.5, f32[1,640]{1,0:T(1,128)} %reshape.22.gain, f32[1,640]{1,0:T(1,128)} %reshape.23.shift, bf16[9,320,640]{2,1,0:T(8,128)(2,1)} %bitcast.4, f32[1,640]{1,0:T(1,128)} %reshape.25.sb, bf16[3,320,640]{2,1,0:T(8,128)(2,1)} %tw.1, f32[1,640]{1,0:T(1,128)} %reshape.26.tb), custom_call_target="tpu_custom_call" | custom-call | tf_op jit(solution)/shard_map/pallas_call | solution.py:321
  101.5 3.7 %copy.9 = bf16[1,1,36,64,640]{4,3,2,1,0:T(8,128)(2,1)} copy(bf16[1,1,36,64,640]{4,3,2,1,0:T(8,128)(2,1)} %bitcast.3) | data formatting | bytes 5898240

commit v2 on v1

--- a/solution.py
+++ b/solution.py
@@ -16,7 +16,10 @@
 QUART = HALF // 4
 R = 4
 NCH = H // R
-NRAW = 3
+NRAW = 4
+SERVE = 5
+KA = 256
+KB = D - KA
 M = R * W
 MEMBERS = 64 * H * W * (D // GROUPS)
 
@@ -28,7 +31,7 @@
 
 def kernel(
     frames, gain, shift, sw, sb, tw, tb, out,
-    xin, xf, sf, so, ss, hid, wts, outv,
+    xin, xf, sf, so, ss, hid, wts, outv, partial,
     st, rs1, tot1, rs2,
     lsem, wsnd, wrcv, st_snd, st_rcv, raw_snd, raw_rcv, sp_snd, sp_rcv, sib_snd, sib_rcv, out_sem,
 ):
@@ -92,6 +95,16 @@
     x_out = wcopy(part(dp, core, pos), 0, x_to)
     x_out.start()
 
+    pre = send(frames.at[pl.ds(0, W), :], xf.at[pl.ds(0, W), :], raw_snd.at[NRAW], raw_rcv.at[NRAW], partner)
+
+    def raw_copy(i):
+        rows = pl.ds(pl.multiple_of(i * M + W, W), M)
+        return send(frames.at[rows, :], xf.at[rows, :], raw_snd.at[i], raw_rcv.at[i], partner)
+
+    def start_raw(i, _):
+        raw_copy(i).start()
+        return 0
+
     load_x.wait()
 
     def add_rows(i, carry):
@@ -109,6 +122,7 @@
         ones[-1].start()
     hid[0:W, :] = jnp.zeros((W, 3 * D), jnp.bfloat16)
     hid[(H + 1) * W:(H + 2) * W, :] = jnp.zeros((W, 3 * D), jnp.bfloat16)
+    x_out.wait_send()
     for c in ones:
         c.wait_recv()
     tot1[...] = st[...] + jnp.sum(rs1[...], axis=0)
@@ -116,6 +130,19 @@
     for k in range(1, 8):
         twos.append(send(tot1, rs2.at[k - 1], st_snd.at[k + 6], st_rcv.at[k + 6], second_group(k)))
         twos[-1].start()
+
+    wcopy(part(other, core, pos), 0, x_to).wait_recv()
+    theirs = 1 - core
+    ring = [
+        wcopy(part(other, core, pos), 1, up),
+        wcopy(part(other, core, pos), 2, down),
+        wcopy(part(other, core, pos), 5, sibling),
+    ]
+    for c in ring:
+        c.start()
+    pre.start()
+    lax.fori_loop(0, 2, start_raw, 0)
+
     for c in twos:
         c.wait_recv()
     total = tot1[...] + jnp.sum(rs2[...], axis=0)
@@ -134,11 +161,11 @@
     inv = lax.rsqrt(per_group[1:2, :] - average * average + 1e-5)
     pair = jnp.concatenate([average, inv, jnp.zeros((6, 128), jnp.float32)], axis=0)
     pair = jnp.dot(pair, spread, precision=lax.Precision.HIGHEST, preferred_element_type=jnp.float32)
-    scale = pair[1:2, :] * gain[...]
+    scale = pair[1:2, :] * gain[...].reshape(1, D)
     half_scale = scale * 0.5
-    half_shift = (shift[...] - pair[0:1, :] * scale) * 0.5
-    bias_s = sb[...]
-    bias_t = tb[...]
+    half_shift = (shift[...].reshape(1, D) - pair[0:1, :] * scale) * 0.5
+    bias_s = sb[...].reshape(1, D)
+    bias_t = tb[...].reshape(1, D)
 
     col = lax.broadcasted_iota(jnp.int32, (W, 128), 0)
     not_first = col > 0
@@ -158,34 +185,35 @@
             hid[to, D + b * 128:D + (b + 1) * 128] = h.astype(jnp.bfloat16)
             hid[to, 2 * D + b * 128:2 * D + (b + 1) * 128] = after.astype(jnp.bfloat16)
 
-    wcopy(part(other, core, pos), 0, x_to).wait_recv()
-    theirs = 1 - core
-    ring = [
-        wcopy(part(other, core, pos), 1, up),
-        wcopy(part(other, core, pos), 2, down),
-        wcopy(part(other, core, pos), 5, sibling),
-    ]
-    for c in ring:
-        c.start()
-
-    pre = send(xin.at[pl.ds(0, W), :], xf.at[pl.ds(0, W), :], raw_snd.at[NRAW], raw_rcv.at[NRAW], partner)
-    pre.start()
-
-    def raw_copy(i):
-        rows = pl.ds(pl.multiple_of(i * M + W, W), M)
-        return send(xin.at[rows, :], xf.at[rows, :], raw_snd.at[i], raw_rcv.at[i], partner)
-
-    def start_raw(i, _):
-        raw_copy(i).start()
-        return 0
-
-    lax.fori_loop(0, NRAW, start_raw, 0)
-
     def own_row(i, _):
         normalise_row(xin, i)
         return 0
 
-    lax.fori_loop(0, H // 2, own_row, 0)
+    lax.fori_loop(0, H, own_row, 0)
+
+    first_ka = pl.multiple_of(dp * KB, 128)
+    first_kb = pl.multiple_of((1 - dp) * KA, 128)
+
+    def taps(i, start, count):
+        left = []
+        for a in range(3):
+            rows = pl.ds(pl.multiple_of(i * M + a * W, W), M)
+            for b in range(3):
+                left.append(hid[rows, pl.ds(pl.multiple_of(b * D + start, 128), count)])
+        left = jnp.concatenate(left, axis=1)
+        right = wts[0:9, pl.ds(start, count), :].reshape(9 * count, D)
+        return jnp.dot(left, right, preferred_element_type=jnp.float32)
+
+    def conv_a(i, _):
+        partial[pl.ds(pl.multiple_of(i * M, M), M), :] = taps(i, first_ka, KA)
+        return 0
+
+    def conv_b(i):
+        rows = pl.ds(pl.multiple_of(i * M, M), M)
+        acc = partial[rows, :] + bias_s + taps(i, first_kb, KB)
+        so[rows, :] = acc.astype(jnp.bfloat16)
+
+    lax.fori_loop(0, SERVE, conv_a, 0)
 
     wcopy(part(other, core, pos - 1), 1, up).wait_recv()
     more = [wcopy(part(other, core, pos - 1, 0, 3), 3, up), wcopy(part(other, core, pos - 1), 6, sibling)]
@@ -195,8 +223,9 @@
     more2 = [wcopy(part(other, core, pos + 1, 3, 3), 4, down), wcopy(part(other, core, pos + 1), 7, sibling)]
     for c in more2:
         c.start()
-
-    lax.fori_loop(H // 2, H, own_row, 0)
+    lax.fori_loop(2, NRAW, start_raw, 0)
+
+    lax.fori_loop(SERVE, NCH, conv_a, 0)
 
     wcopy(part(other, core, pos + 2, 0, 3), 3, up).wait_recv()
     last = [wcopy(part(other, core, pos + 2, 0, 3), 8, sibling)]
@@ -214,14 +243,9 @@
     ):
         wcopy(piece, i, sibling).wait_recv()
 
-    def conv(i, dst):
-        acc = jnp.broadcast_to(bias_s, (M, D))
-        for a in range(3):
-            rows = pl.ds(pl.multiple_of(i * M + a * W, W), M)
-            acc = acc + jnp.dot(
-                hid[rows, :], wts[3 * a:3 * a + 3].reshape(3 * D, D), preferred_element_type=jnp.float32
-            )
-        dst[pl.ds(pl.multiple_of(i * M, M), M), :] = acc.astype(jnp.bfloat16)
+    def conv_far(i):
+        acc = taps(i, 0, D) + bias_s
+        sf[pl.ds(pl.multiple_of(i * M, M), M), :] = acc.astype(jnp.bfloat16)
 
     def chunk(ref, i):
         return ref.at[pl.ds(pl.multiple_of(i * M, M), M), :]
@@ -233,7 +257,7 @@
         return send(chunk(so, i), chunk(sf, i), sp_snd.at[i], sp_rcv.at[i], partner)
 
     def shared_chunk(i, _):
-        conv(i, so)
+        conv_b(i)
         to_partner(i).start()
         to_sibling(i).start()
         return 0
@@ -241,7 +265,7 @@
     lax.fori_loop(NRAW, NCH, shared_chunk, 0)
 
     def own_chunk(i, _):
-        conv(i, so)
+        conv_b(i)
         to_sibling(i).start()
         return 0
 
@@ -276,7 +300,7 @@
             return 0
 
         lax.fori_loop(0, R, one, 0)
-        conv(i, sf)
+        conv_far(i)
         temporal(i)
         return 0
 
@@ -289,7 +313,7 @@
 
     lax.fori_loop(NRAW, NCH, sent_chunk, 0)
 
-    for c in ones + twos + [x_out] + ring + more + more2 + last + [pre]:
+    for c in ones + twos + ring + more + more2 + last + [pre]:
         c.wait_send()
 
     def drain_raw(i, _):
@@ -313,7 +337,6 @@
 
 
 def shards(frames, norm_gain, norm_shift, spatial_weight, spatial_bias, temporal_weight, temporal_bias):
-    row = lambda v: v.reshape(1, D)
     vm = pl.BlockSpec(memory_space=pltpu.VMEM)
     hbm = pl.BlockSpec(memory_space=pl.ANY)
     dma = pltpu.SemaphoreType.DMA
@@ -332,6 +355,7 @@
             pltpu.VMEM(((H + 2) * W, 3 * D), bf),
             pltpu.VMEM((12, D, D), bf),
             pltpu.VMEM((H * W, D), bf),
+            pltpu.VMEM((H * W, D), jnp.float32),
             pltpu.VMEM((2, D), jnp.float32),
             pltpu.VMEM((7, 2, D), jnp.float32),
             pltpu.VMEM((2, D), jnp.float32),
@@ -344,8 +368,8 @@
             collective_id=0, has_side_effects=True, vmem_limit_bytes=56 * 2**20
         ),
     )(
-        frames.reshape(H * W, D), row(norm_gain), row(norm_shift),
-        spatial_weight.reshape(9, HALF, D), row(spatial_bias), temporal_weight, row(temporal_bias),
+        frames.reshape(H * W, D), norm_gain, norm_shift,
+        spatial_weight.reshape(9, HALF, D), spatial_bias, temporal_weight, temporal_bias,
     )
     return result.reshape(1, 1, H, W, D)
 

time: 107 us -> 91.6 us (0.86); the launches traced: 105 us -> 91.4 us
  Pallas kernels: 96.4 us -> 87.7 us
  local copies, waits for them, and re-layouts: 8.75 us -> 3.69 us
    pallas_call x1, Pallas kernels: 96.4 us -> 87.7 us  [shards(): pl.pallas_call(kernel, out_shape=jax.ShapeDtypeStruct((H * W, D), bf), in...]
    reshape x4 -> x0, local copies, waits for them, and re-layouts: 5.06 us -> none  [shards(): row = lambda v: v.reshape(1, D)]
where the time goes in v2:
time: 91.6 us; the launch traced here: 91.4 us
  Pallas kernels  87.7 us (96%)
  local copies, waits for them, and re-layouts  3.69 us (4%)
    pallas_call x1, Pallas kernels, shards(): pl.pallas_call(kernel, out_shape=jax.ShapeDtypeStruct((H * W, D), bf), in...  87.7 us
    unnamed x1, local copies, waits for them, and re-layouts  3.69 us

profile of v2, /device:TPU:0, one launch (start us, length us, event | category | flops | bytes accessed | tf_op | source)
XLA Modules:
  0.0 91.4 jit_solution(9515137490912482999)
XLA Ops:
  0.0 87.7 %shard_map.73 = bf16[2304,640]{1,0:T(8,128)(2,1)} custom-call(bf16[2304,640]{1,0:T(8,128)(2,1)} %bitcast.5, f32[640]{0:T(1024)} %gain.1, f32[640]{0:T(1024)} %shift.1, bf16[9,320,640]{2,1,0:T(8,128)(2,1)} %bitcast.4, f32[640]{0:T(1024)} %sb.1, bf16[3,320,640]{2,1,0:T(8,128)(2,1)} %tw.1, f32[640]{0:T(1024)} %tb.1), custom_call_target="tpu_custom_call" | custom-call | tf_op jit(solution)/shard_map/pallas_call | solution.py:344
  87.7 3.7 %copy.9 = bf16[1,1,36,64,640]{4,3,2,1,0:T(8,128)(2,1)} copy(bf16[1,1,36,64,640]{4,3,2,1,0:T(8,128)(2,1)} %bitcast.3) | data formatting | bytes 5898240

commit v3 on v2

--- a/solution.py
+++ b/solution.py
@@ -31,9 +31,9 @@
 
 def kernel(
     frames, gain, shift, sw, sb, tw, tb, out,
-    xin, xf, sf, so, ss, hid, wts, outv, partial,
+    xin, xf, sf, so, ss, hid, wts, partial,
     st, rs1, tot1, rs2,
-    lsem, wsnd, wrcv, st_snd, st_rcv, raw_snd, raw_rcv, sp_snd, sp_rcv, sib_snd, sib_rcv, out_sem,
+    lsem, wsnd, wrcv, st_snd, st_rcv, raw_snd, raw_rcv, sp_snd, sp_rcv, sib_snd, sib_rcv,
 ):
     dp = lax.axis_index("dp")
     tm = lax.axis_index("tm")
@@ -274,9 +274,6 @@
     far_tap = 9 + 2 * core
     near_tap = 11 - 2 * core
 
-    def store(i):
-        return pltpu.make_async_copy(chunk(outv, i), chunk(out, i), out_sem.at[i])
-
     def temporal(i):
         to_sibling(i).wait_recv()
         rows = pl.ds(pl.multiple_of(i * M, M), M)
@@ -286,8 +283,7 @@
         far = sf[rows, :]
         far = jnp.where(valid, far, jnp.zeros_like(far))
         acc = acc + jnp.dot(far, wts[far_tap], preferred_element_type=jnp.float32)
-        outv[rows, :] = acc.astype(jnp.bfloat16)
-        store(i).start()
+        out[rows, :] = acc.astype(jnp.bfloat16)
 
     pre.wait_recv()
     normalise_row(xf, 0)
@@ -330,7 +326,6 @@
 
     def drain_all(i, _):
         to_sibling(i).wait_send()
-        store(i).wait()
         return 0
 
     lax.fori_loop(0, NCH, drain_all, 0)
@@ -343,9 +338,9 @@
     bf = jnp.bfloat16
     result = pl.pallas_call(
         kernel,
-        out_shape=jax.ShapeDtypeStruct((H * W, D), bf),
+        out_shape=pltpu.VMEM((H * W, D), bf),
         in_specs=[hbm, vm, vm, hbm, vm, hbm, vm],
-        out_specs=hbm,
+        out_specs=vm,
         scratch_shapes=[
             pltpu.VMEM((H * W, D), bf),
             pltpu.VMEM(((NRAW * R + 1) * W, D), bf),
@@ -354,7 +349,6 @@
             pltpu.VMEM((H * W, D), bf),
             pltpu.VMEM(((H + 2) * W, 3 * D), bf),
             pltpu.VMEM((12, D, D), bf),
-            pltpu.VMEM((H * W, D), bf),
             pltpu.VMEM((H * W, D), jnp.float32),
             pltpu.VMEM((2, D), jnp.float32),
             pltpu.VMEM((7, 2, D), jnp.float32),
@@ -362,7 +356,7 @@
             pltpu.VMEM((7, 2, D), jnp.float32),
             dma((3,)), dma((10,)), dma((10,)), dma((14,)), dma((14,)),
             dma((NRAW + 1,)), dma((NRAW + 1,)), dma((NCH,)), dma((NCH,)),
-            dma((NCH,)), dma((NCH,)), dma((NCH,)),
+            dma((NCH,)), dma((NCH,)),
         ],
         compiler_params=pltpu.CompilerParams(
             collective_id=0, has_side_effects=True, vmem_limit_bytes=56 * 2**20

time: 91.6 us -> 88.8 us (0.969)
  local copies, waits for them, and re-layouts: 3.69 us -> 1.6 us
    unnamed x1, local copies, waits for them, and re-layouts: 3.69 us -> 1.6 us
where the time goes in v3:
time: 88.8 us; the launch traced here: 88.6 us
  Pallas kernels  87 us (98%)
  local copies, waits for them, and re-layouts  1.6 us (2%)
    pallas_call x1, Pallas kernels, shards(): pl.pallas_call(kernel, out_shape=pltpu.VMEM((H * W, D), bf), in_specs=[hb...  87 us

profile of v3, /device:TPU:0, one launch (start us, length us, event | category | flops | bytes accessed | tf_op | source)
XLA Modules:
  0.0 88.6 jit_solution(10999450042430202262)
XLA Ops:
  0.0 87.0 %shard_map.73 = bf16[2304,640]{1,0:T(8,128)(2,1)S(1)} custom-call(bf16[2304,640]{1,0:T(8,128)(2,1)} %bitcast.5, f32[640]{0:T(1024)} %gain.1, f32[640]{0:T(1024)} %shift.1, bf16[9,320,640]{2,1,0:T(8,128)(2,1)} %bitcast.4, f32[640]{0:T(1024)} %sb.1, bf16[3,320,640]{2,1,0:T(8,128)(2,1)} %tw.1, f32[640]{0:T(1024)} %tb.1), custom_call_target="tpu_custom_call" | custom-call | tf_op jit(solution)/shard_map/pallas_call | solution.py:339
  87.0 1.6 %copy.9 = bf16[1,1,36,64,640]{4,3,2,1,0:T(8,128)(2,1)} copy(bf16[1,1,36,64,640]{4,3,2,1,0:T(8,128)(2,1)S(1)} %bitcast.3) | data formatting | bytes 5898240

commit v4 on v3

--- a/solution.py
+++ b/solution.py
@@ -17,7 +17,8 @@
 R = 4
 NCH = H // R
 NRAW = 4
-SERVE = 5
+BURST = 2
+NSUB = 3
 KA = 256
 KB = D - KA
 M = R * W
@@ -83,17 +84,59 @@
             src_ref=src, dst_ref=dst, send_sem=ssem, recv_sem=rsem, device_id=who, device_id_type=MESH
         )
 
-    def part(half, owner_core, q, first=0, count=6):
+    def part(half, owner_core, q, first, count):
         rows = pl.ds(pl.multiple_of(half * HALF + lax.rem(q + 4, 4) * QUART, 16), QUART)
         return wts.at[pl.ds(owner_core * 6 + first, count), rows, :]
 
-    def wcopy(piece, i, who):
-        return send(piece, piece, wsnd.at[i], wrcv.at[i], who)
+    def wcopy(piece, k, i, who):
+        return send(piece, piece, wsnd.at[k, i], wrcv.at[k, i], who)
+
+    sent = []
+
+    def go(copy):
+        copy.start()
+        sent.append(copy)
+
+    def weights_x(k):
+        go(wcopy(part(dp, core, pos, 2 * k, 2), k, 0, x_to))
+
+    def weights_ring(k):
+        piece = part(other, core, pos, 2 * k, 2)
+        wcopy(piece, k, 0, x_to).wait_recv()
+        go(wcopy(piece, k, 1, up))
+        go(wcopy(piece, k, 2, down))
+        go(wcopy(piece, k, 5, sibling))
+
+    def weights_on(k):
+        piece = part(other, core, pos - 1, 2 * k, 2)
+        wcopy(piece, k, 1, up).wait_recv()
+        go(wcopy(part(other, core, pos - 1, 2 * k, 1), k, 3, up))
+        go(wcopy(piece, k, 6, sibling))
+        piece = part(other, core, pos + 1, 2 * k, 2)
+        wcopy(piece, k, 2, down).wait_recv()
+        go(wcopy(part(other, core, pos + 1, 2 * k + 1, 1), k, 4, down))
+        go(wcopy(piece, k, 7, sibling))
+
+    def weights_last(k):
+        piece = part(other, core, pos + 2, 2 * k, 1)
+        wcopy(piece, k, 3, up).wait_recv()
+        go(wcopy(piece, k, 8, sibling))
+        piece = part(other, core, pos + 2, 2 * k + 1, 1)
+        wcopy(piece, k, 4, down).wait_recv()
+        go(wcopy(piece, k, 9, sibling))
+
+    def weights_near(k):
+        theirs = 1 - core
+        their_pos = y * (1 - theirs) + z * theirs
+        for i, (shift_by, first, count) in enumerate((
+            (0, 2 * k, 2), (-1, 2 * k, 2), (1, 2 * k, 2), (2, 2 * k, 1), (2, 2 * k + 1, 1),
+        )):
+            wcopy(part(other, theirs, their_pos + shift_by, first, count), k, 5 + i, sibling).wait_recv()
 
     load_s.wait()
     load_t.wait()
-    x_out = wcopy(part(dp, core, pos), 0, x_to)
-    x_out.start()
+    for k in range(NSUB):
+        weights_x(k)
 
     pre = send(frames.at[pl.ds(0, W), :], xf.at[pl.ds(0, W), :], raw_snd.at[NRAW], raw_rcv.at[NRAW], partner)
 
@@ -122,7 +165,7 @@
         ones[-1].start()
     hid[0:W, :] = jnp.zeros((W, 3 * D), jnp.bfloat16)
     hid[(H + 1) * W:(H + 2) * W, :] = jnp.zeros((W, 3 * D), jnp.bfloat16)
-    x_out.wait_send()
+    weights_ring(0)
     for c in ones:
         c.wait_recv()
     tot1[...] = st[...] + jnp.sum(rs1[...], axis=0)
@@ -131,20 +174,12 @@
         twos.append(send(tot1, rs2.at[k - 1], st_snd.at[k + 6], st_rcv.at[k + 6], second_group(k)))
         twos[-1].start()
 
-    wcopy(part(other, core, pos), 0, x_to).wait_recv()
-    theirs = 1 - core
-    ring = [
-        wcopy(part(other, core, pos), 1, up),
-        wcopy(part(other, core, pos), 2, down),
-        wcopy(part(other, core, pos), 5, sibling),
-    ]
-    for c in ring:
-        c.start()
-    pre.start()
-    lax.fori_loop(0, 2, start_raw, 0)
-
+    weights_ring(1)
     for c in twos:
         c.wait_recv()
+    pre.start()
+    lax.fori_loop(0, BURST, start_raw, 0)
+    weights_ring(2)
     total = tot1[...] + jnp.sum(rs2[...], axis=0)
 
     ch = lax.broadcasted_iota(jnp.int32, (D, 128), 0)
@@ -189,7 +224,10 @@
         normalise_row(xin, i)
         return 0
 
-    lax.fori_loop(0, H, own_row, 0)
+    lax.fori_loop(0, H // 2, own_row, 0)
+    weights_on(0)
+    lax.fori_loop(H // 2, H, own_row, 0)
+    weights_on(1)
 
     first_ka = pl.multiple_of(dp * KB, 128)
     first_kb = pl.multiple_of((1 - dp) * KA, 128)
@@ -213,35 +251,18 @@
         acc = partial[rows, :] + bias_s + taps(i, first_kb, KB)
         so[rows, :] = acc.astype(jnp.bfloat16)
 
-    lax.fori_loop(0, SERVE, conv_a, 0)
-
-    wcopy(part(other, core, pos - 1), 1, up).wait_recv()
-    more = [wcopy(part(other, core, pos - 1, 0, 3), 3, up), wcopy(part(other, core, pos - 1), 6, sibling)]
-    for c in more:
-        c.start()
-    wcopy(part(other, core, pos + 1), 2, down).wait_recv()
-    more2 = [wcopy(part(other, core, pos + 1, 3, 3), 4, down), wcopy(part(other, core, pos + 1), 7, sibling)]
-    for c in more2:
-        c.start()
-    lax.fori_loop(2, NRAW, start_raw, 0)
-
-    lax.fori_loop(SERVE, NCH, conv_a, 0)
-
-    wcopy(part(other, core, pos + 2, 0, 3), 3, up).wait_recv()
-    last = [wcopy(part(other, core, pos + 2, 0, 3), 8, sibling)]
-    last[0].start()
-    wcopy(part(other, core, pos + 2, 3, 3), 4, down).wait_recv()
-    last.append(wcopy(part(other, core, pos + 2, 3, 3), 9, sibling))
-    last[1].start()
-    their_pos = y * (1 - theirs) + z * theirs
-    for piece, i in (
-        (part(other, theirs, their_pos), 5),
-        (part(other, theirs, their_pos - 1), 6),
-        (part(other, theirs, their_pos + 1), 7),
-        (part(other, theirs, their_pos + 2, 0, 3), 8),
-        (part(other, theirs, their_pos + 2, 3, 3), 9),
-    ):
-        wcopy(piece, i, sibling).wait_recv()
+    lax.fori_loop(0, 1, conv_a, 0)
+    weights_on(2)
+    lax.fori_loop(BURST, NRAW, start_raw, 0)
+    lax.fori_loop(1, 3, conv_a, 0)
+    weights_last(0)
+    lax.fori_loop(3, 5, conv_a, 0)
+    weights_last(1)
+    lax.fori_loop(5, 7, conv_a, 0)
+    weights_last(2)
+    lax.fori_loop(7, NCH, conv_a, 0)
+    for k in range(NSUB):
+        weights_near(k)
 
     def conv_far(i):
         acc = taps(i, 0, D) + bias_s
@@ -309,7 +330,7 @@
 
     lax.fori_loop(NRAW, NCH, sent_chunk, 0)
 
-    for c in ones + twos + ring + more + more2 + last + [pre]:
+    for c in ones + twos + sent + [pre]:
         c.wait_send()
 
     def drain_raw(i, _):
@@ -354,7 +375,7 @@
             pltpu.VMEM((7, 2, D), jnp.float32),
             pltpu.VMEM((2, D), jnp.float32),
             pltpu.VMEM((7, 2, D), jnp.float32),
-            dma((3,)), dma((10,)), dma((10,)), dma((14,)), dma((14,)),
+            dma((3,)), dma((NSUB, 10)), dma((NSUB, 10)), dma((14,)), dma((14,)),
             dma((NRAW + 1,)), dma((NRAW + 1,)), dma((NCH,)), dma((NCH,)),
             dma((NCH,)), dma((NCH,)),
         ],

time: 88.8 us -> 93 us (1.047)
  Pallas kernels: 87 us -> 91.3 us
    pallas_call x1, Pallas kernels: 87 us -> 91.3 us  [shards(): pl.pallas_call(kernel, out_shape=pltpu.VMEM((H * W, D), bf), in_specs=[hb...]
where the time goes in v4:
time: 93 us; the launch traced here: 92.9 us
  Pallas kernels  91.3 us (98%)
  local copies, waits for them, and re-layouts  1.6 us (2%)
    pallas_call x1, Pallas kernels, shards(): pl.pallas_call(kernel, out_shape=pltpu.VMEM((H * W, D), bf), in_specs=[hb...  91.3 us

profile of v4, /device:TPU:0, one launch (start us, length us, event | category | flops | bytes accessed | tf_op | source)
XLA Modules:
  0.0 92.9 jit_solution(11571966272910328558)
XLA Ops:
  0.0 91.3 %shard_map.73 = bf16[2304,640]{1,0:T(8,128)(2,1)S(1)} custom-call(bf16[2304,640]{1,0:T(8,128)(2,1)} %bitcast.5, f32[640]{0:T(1024)} %gain.1, f32[640]{0:T(1024)} %shift.1, bf16[9,320,640]{2,1,0:T(8,128)(2,1)} %bitcast.4, f32[640]{0:T(1024)} %sb.1, bf16[3,320,640]{2,1,0:T(8,128)(2,1)} %tw.1, f32[640]{0:T(1024)} %tb.1), custom_call_target="tpu_custom_call" | custom-call | tf_op jit(solution)/shard_map/pallas_call | solution.py:360
  91.3 1.6 %copy.9 = bf16[1,1,36,64,640]{4,3,2,1,0:T(8,128)(2,1)} copy(bf16[1,1,36,64,640]{4,3,2,1,0:T(8,128)(2,1)S(1)} %bitcast.3) | data formatting | bytes 5898240

commit v5 on v3

--- a/solution.py
+++ b/solution.py
@@ -67,9 +67,9 @@
     mine = pl.ds(pl.multiple_of(dp * HALF, 16), HALF)
     load_s = pltpu.make_async_copy(sw, wts.at[pl.ds(0, 9), mine, :], lsem.at[1])
     load_t = pltpu.make_async_copy(tw, wts.at[pl.ds(9, 3), mine, :], lsem.at[2])
-    load_x.start()
     load_s.start()
     load_t.start()
+    load_x.start()
 
     barrier = pltpu.get_barrier_semaphore()
     greet = [sibling, partner, x_to, x_from, up, down]

time: 88.8 us -> 88 us (level)
  no operation moved by 1% of the time
where the time goes in v5:
time: 88 us; the launch traced here: 87.8 us
  Pallas kernels  86.2 us (98%)
  local copies, waits for them, and re-layouts  1.6 us (2%)
    pallas_call x1, Pallas kernels, shards(): pl.pallas_call(kernel, out_shape=pltpu.VMEM((H * W, D), bf), in_specs=[hb...  86.2 us

profile of v5, /device:TPU:0, one launch (start us, length us, event | category | flops | bytes accessed | tf_op | source)
XLA Modules:
  0.0 87.8 jit_solution(14763830662837056339)
XLA Ops:
  0.0 86.2 %shard_map.73 = bf16[2304,640]{1,0:T(8,128)(2,1)S(1)} custom-call(bf16[2304,640]{1,0:T(8,128)(2,1)} %bitcast.5, f32[640]{0:T(1024)} %gain.1, f32[640]{0:T(1024)} %shift.1, bf16[9,320,640]{2,1,0:T(8,128)(2,1)} %bitcast.4, f32[640]{0:T(1024)} %sb.1, bf16[3,320,640]{2,1,0:T(8,128)(2,1)} %tw.1, f32[640]{0:T(1024)} %tb.1), custom_call_target="tpu_custom_call" | custom-call | tf_op jit(solution)/shard_map/pallas_call | solution.py:339
  86.2 1.6 %copy.9 = bf16[1,1,36,64,640]{4,3,2,1,0:T(8,128)(2,1)} copy(bf16[1,1,36,64,640]{4,3,2,1,0:T(8,128)(2,1)S(1)} %bitcast.3) | data formatting | bytes 5898240

commit v6 on v5

--- a/solution.py
+++ b/solution.py
@@ -69,7 +69,6 @@
     load_t = pltpu.make_async_copy(tw, wts.at[pl.ds(9, 3), mine, :], lsem.at[2])
     load_s.start()
     load_t.start()
-    load_x.start()
 
     barrier = pltpu.get_barrier_semaphore()
     greet = [sibling, partner, x_to, x_from, up, down]
@@ -94,6 +93,7 @@
     load_t.wait()
     x_out = wcopy(part(dp, core, pos), 0, x_to)
     x_out.start()
+    load_x.start()
 
     pre = send(frames.at[pl.ds(0, W), :], xf.at[pl.ds(0, W), :], raw_snd.at[NRAW], raw_rcv.at[NRAW], partner)
 

time: 88 us -> 88 us (level)
  no operation moved by 1% of the time
where the time goes in v6:
time: 88 us; the launch traced here: 87.8 us
  Pallas kernels  86.2 us (98%)
  local copies, waits for them, and re-layouts  1.6 us (2%)
    pallas_call x1, Pallas kernels, shards(): pl.pallas_call(kernel, out_shape=pltpu.VMEM((H * W, D), bf), in_specs=[hb...  86.2 us

profile of v6, /device:TPU:0, one launch (start us, length us, event | category | flops | bytes accessed | tf_op | source)
XLA Modules:
  0.0 87.8 jit_solution(1215278430166854542)
XLA Ops:
  0.0 86.2 %shard_map.73 = bf16[2304,640]{1,0:T(8,128)(2,1)S(1)} custom-call(bf16[2304,640]{1,0:T(8,128)(2,1)} %bitcast.5, f32[640]{0:T(1024)} %gain.1, f32[640]{0:T(1024)} %shift.1, bf16[9,320,640]{2,1,0:T(8,128)(2,1)} %bitcast.4, f32[640]{0:T(1024)} %sb.1, bf16[3,320,640]{2,1,0:T(8,128)(2,1)} %tw.1, f32[640]{0:T(1024)} %tb.1), custom_call_target="tpu_custom_call" | custom-call | tf_op jit(solution)/shard_map/pallas_call | solution.py:339
  86.2 1.6 %copy.9 = bf16[1,1,36,64,640]{4,3,2,1,0:T(8,128)(2,1)} copy(bf16[1,1,36,64,640]{4,3,2,1,0:T(8,128)(2,1)S(1)} %bitcast.3) | data formatting | bytes 5898240
